TPU v7x, 256 devices: a whole 4x4x8 slice. The times are simulated.
256 devices in a mesh: tm: 4 (over y), height: 4 (over x), width: 16 (over z, core).
Axes of the slice: x: 4, y: 4, z: 8, core: 2. Of those that a mesh axis runs over, the one named last changes fastest.
Arguments:
- features: bfloat16 [16, 32, 160, 384], P('tm', 'height', 'width'), may hold values from -6 to 6
- first_gain: float32 [384], replicated, may hold values from 0.5 to 2
- first_kernel: bfloat16 [27, 384, 384], P(None, ('height', 'width')), may hold values from -0.0625 to 0.0625
- first_bias: float32 [384], replicated, may hold values from -3 to 3
- second_gain: float32 [384], replicated, may hold values from 0.5 to 2
- second_kernel: bfloat16 [27, 384, 384], P(None, ('height', 'width')), may hold values from -0.0625 to 0.0625
- second_bias: float32 [384], replicated, may hold values from -3 to 3
Outputs:
- block_out: bfloat16 [16, 32, 160, 384], P('tm', 'height', 'width')
All inputs are finite; a program needn't handle non-finite values.
Results may differ from a plain program's by a relative error of at most 0.012.
Values may be sent and summed in bfloat16 or wider, within the bound.
No kernel may reach another device: no remote copies, remote signals or barrier semaphores. Data moves between devices by JAX's collectives and lax.ppermute only.
A program may use at most 128 MiB of HBM per device.

v0:
```python
import jax
import jax.numpy as jnp
from jax import lax
from jax.sharding import PartitionSpec as P


def passed_along(x, axis, by):
    devices = lax.axis_size(axis)
    pairs = [(i, i + by) for i in range(devices) if 0 <= i + by < devices]
    return lax.ppermute(x, axis, pairs)


def extended(x, sides, width):
    for axis, dim in sides:
        devices, length = (lax.axis_size(axis), x.shape[dim])
        up = [(i, (i + 1) % devices) for i in range(devices - 1)]
        down = [(j, i) for i, j in up]
        last = lax.slice_in_dim(x, length - width, length, axis=dim)
        first = lax.slice_in_dim(x, 0, width, axis=dim)
        before = lax.ppermute(last, axis, up)
        after = lax.ppermute(first, axis, down)
        x = jnp.concatenate([before, x, after], axis=dim)
    return x


def activate(volume, gain):
    values = volume.astype(jnp.float32)
    square_mean = jnp.mean(values * values, axis=-1, keepdims=True)
    normed = values * lax.rsqrt(square_mean + 1e-06) * gain
    return jax.nn.silu(normed).astype(jnp.bfloat16)


def make_folder(widened, frames, rows, cols):

    def fold_piece(total, piece, start):
        count_in = piece.shape[1]
        for step_t in range(3):
            for step_h in range(3):
                for step_w in range(3):
                    window = widened[
                        step_t : step_t + frames, step_h : step_h + rows, step_w : step_w + cols
                    ]
                    total = total + jnp.dot(
                        window.reshape(-1, count_in),
                        piece[9 * step_t + 3 * step_h + step_w],
                        preferred_element_type=jnp.float32,
                    )
        return total

    return fold_piece


def convolve(widened, kernel, bias, frames, rows, cols):
    out_chans = kernel.shape[2]
    empty = jnp.zeros((frames * rows * cols, out_chans), jnp.float32)
    fold_piece = make_folder(widened, frames, rows, cols)
    row_kernel = lax.all_gather(kernel, "width", axis=1, tiled=True)
    total = fold_piece(
        empty, lax.all_gather(row_kernel, "height", axis=1, tiled=True), jnp.int32(0)
    )
    return total.reshape(frames, rows, cols, out_chans) + bias


def widen(active):
    earlier = passed_along(active[-2:], "tm", 1)
    tall = jnp.concatenate([earlier, active], axis=0)
    return extended(tall, (("height", 1), ("width", 2)), 1)


def on_device(
    features, first_gain, first_kernel, first_bias, second_gain, second_kernel, second_bias
):
    frames, rows, cols, chans = features.shape
    first_active = activate(features, first_gain)
    middle = convolve(widen(first_active), first_kernel, first_bias, frames, rows, cols).astype(
        jnp.bfloat16
    )
    second_active = activate(middle, second_gain)
    second_wide = widen(second_active)
    summed = convolve(
        second_wide, second_kernel, second_bias, frames, rows, cols
    ) + features.astype(jnp.float32)
    return summed.astype(jnp.bfloat16)


def solution(mesh):
    placed = (
        P("tm", "height", "width", None),
        P(),
        P(None, ("height", "width"), None),
        P(),
        P(),
        P(None, ("height", "width"), None),
        P(),
    )
    return jax.shard_map(
        on_device,
        mesh=mesh,
        in_specs=placed,
        out_specs=P("tm", "height", "width", None),
        check_vma=False,
    )
```

profile of v0, /device:TPU:1, one launch (start us, length us, event | category | flops | bytes accessed | tf_op | source)
XLA Modules:
  0.0 329.2 jit_solution(13650596367216335500)
XLA Ops:
  8.1 45.3 %all-gather.5.cloned.1.call-done = bf16[27,96,384]{2,0,1:T(8,128)(2,1)} async-done(((bf16[27,6,384]{2,0,1:T(8,128)(2,1)}), bf16[27,96,384]{2,0,1:T(8,128)(2,1)}) %all-gather.5.cloned.1.call-update) | async-done | bytes 1990672 | tf_op jit(solution)/shard_map/all_gather | solution.py:57
  53.4 3.7 %copy.15 = bf16[27,96,384]{2,1,0:T(8,128)(2,1)} copy(bf16[27,96,384]{2,0,1:T(8,128)(2,1)} %all-gather.5.cloned.1.call-done) | data formatting | bytes 3981312 | tf_op jit(solution)/shard_map/all_gather | solution.py:57
  57.1 36.5 %all-gather.9.cloned.1.call-done = bf16[27,96,384]{2,0,1:T(8,128)(2,1)} async-done(((bf16[27,6,384]{2,0,1:T(8,128)(2,1)}), bf16[27,96,384]{2,0,1:T(8,128)(2,1)}) %all-gather.9.cloned.1.call-update) | async-done | bytes 1990672 | tf_op jit(solution)/shard_map/all_gather | solution.py:57
  93.6 3.7 %copy.16 = bf16[27,96,384]{2,1,0:T(8,128)(2,1)} copy(bf16[27,96,384]{2,0,1:T(8,128)(2,1)} %all-gather.9.cloned.1.call-done) | data formatting | bytes 3981312 | tf_op jit(solution)/shard_map/all_gather | solution.py:57
  97.9 3.1 collective-permute-start
  101.8 3.2 collective-permute-done
  106.3 4.0 %collective-permute-start.1 = (bf16[6,1,10,384]{3,2,1,0:T(8,128)(2,1)S(1)}, bf16[6,1,10,384]{3,2,1,0:T(8,128)(2,1)S(1)}, u32[]{:S(2)}, u32[]{:S(2)}) collective-permute-start(bf16[6,1,10,384]{3,2,1,0:T(8,128)(2,1)S(1)} %get-tuple-element.71), channel_id=1, source_target_pairs={{0,16},{16,32},{32,48},{1,17},{17,33},{33,49},{2,18},{18,34},{34,5... | collective-permute-start | bytes 138248 | tf_op jit(solution)/shard_map/ppermute | solution.py:20
  114.2 4.9 %collective-permute-start.3 = (bf16[6,10,1,384]{3,2,1,0:T(2,128)(2,1)}, bf16[6,10,1,384]{3,2,1,0:T(2,128)(2,1)S(1)}, u32[]{:S(2)}, u32[]{:S(2)}) collective-permute-start(bf16[6,10,1,384]{3,2,1,0:T(2,128)(2,1)} %get-tuple-element.47), channel_id=1, source_target_pairs={{0,1},{1,2},{2,3},{3,4},{4,5},{5,6},{6,7},{7,8},{8,9},{9,10},{10,1... | collective-permute-start | bytes 138248 | tf_op jit(solution)/shard_map/ppermute | solution.py:20
  119.1 2.1 collective-permute-start.4
  127.2 2.3 fusion.32
  129.4 1.8 reshape.211
  131.2 1.8 reshape.197
  133.0 1.8 reshape.199
  134.8 1.8 reshape.200
  136.6 1.8 reshape.202
  138.4 1.8 reshape.203
  140.2 1.8 reshape.205
  142.0 1.8 reshape.206
  143.8 1.8 reshape.208
  145.6 1.8 reshape.209
  151.7 24.5 %all-gather.7.cloned.1.call-done = bf16[27,384,384]{2,1,0:T(8,128)(2,1)} async-done(((bf16[27,96,384]{2,1,0:T(8,128)(2,1)}), bf16[27,384,384]{2,1,0:T(8,128)(2,1)}) %all-gather.7.cloned.1.call-update) | async-done | bytes 7962640 | tf_op jit(solution)/shard_map/all_gather | solution.py:59
  176.2 1.6 fusion.23
  177.8 1.8 fusion.24
  179.5 1.4 convolution_add_fusion.49
  181.0 1.5 convolution_add_fusion.48
  182.4 1.5 convolution_add_fusion.47
  183.9 1.3 convolution_add_fusion.46
  186.4 1.3 convolution_add_fusion.42
  194.3 3.3 collective-permute-start.5
  197.6 3.5 %collective-permute-done.5 = bf16[2,8,10,384]{3,2,1,0:T(8,128)(2,1)S(1)} collective-permute-done((bf16[2,8,10,384]{3,2,1,0:T(8,128)(2,1)S(1)}, bf16[2,8,10,384]{3,2,1,0:T(8,128)(2,1)S(1)}, u32[]{:S(2)}, u32[]{:S(2)}) %collective-permute-start.5) | collective-permute-done | bytes 122912 | tf_op jit(solution)/shard_map/ppermute | solution.py:10
  202.5 4.2 %collective-permute-start.6 = (bf16[6,1,10,384]{3,2,1,0:T(8,128)(2,1)S(1)}, bf16[6,1,10,384]{3,2,1,0:T(8,128)(2,1)S(1)}, u32[]{:S(2)}, u32[]{:S(2)}) collective-permute-start(bf16[6,1,10,384]{3,2,1,0:T(8,128)(2,1)S(1)} %get-tuple-element.65), channel_id=1, source_target_pairs={{0,16},{16,32},{32,48},{1,17},{17,33},{33,49},{2,18},{18,34},{34,5... | collective-permute-start | bytes 138248 | tf_op jit(solution)/shard_map/ppermute | solution.py:20
  210.1 5.8 %collective-permute-start.8 = (bf16[6,10,1,384]{3,2,1,0:T(2,128)(2,1)}, bf16[6,10,1,384]{3,2,1,0:T(2,128)(2,1)}, u32[]{:S(2)}, u32[]{:S(2)}) collective-permute-start(bf16[6,10,1,384]{3,2,1,0:T(2,128)(2,1)} %get-tuple-element.25), channel_id=1, source_target_pairs={{0,1},{1,2},{2,3},{3,4},{4,5},{5,6},{6,7},{7,8},{8,9},{9,10},{10,1... | collective-permute-start | bytes 138248 | tf_op jit(solution)/shard_map/ppermute | solution.py:20
  215.9 1.9 collective-permute-start.9
  220.1 42.1 %all-gather.11.cloned.1.call-done = bf16[27,384,384]{2,1,0:T(8,128)(2,1)} async-done(((bf16[27,96,384]{2,1,0:T(8,128)(2,1)}), bf16[27,384,384]{2,1,0:T(8,128)(2,1)}) %all-gather.11.cloned.1.call-update) | async-done | bytes 7962640 | tf_op jit(solution)/shard_map/all_gather | solution.py:59
  262.2 1.4 fusion.22
  263.6 1.8 reshape.232
  266.2 1.8 reshape.241
  268.8 1.8 reshape.249
  270.5 1.6 maximum_maximum_fusion.1
  272.1 1.8 fusion.30
  273.9 1.8 reshape.239
  275.7 1.9 fusion.31
  277.6 1.9 reshape.225
  279.4 1.8 reshape.227
  281.2 1.8 reshape.228
  283.0 1.8 reshape.230
  284.8 1.8 reshape.231
  286.6 1.8 reshape.233
  288.4 1.8 reshape.234
  290.1 1.8 reshape.236
  291.9 1.8 reshape.237
  293.7 1.8 reshape.240
  295.5 1.8 reshape.242
  297.3 1.8 reshape.243
  300.3 1.6 fusion.21
  301.9 1.4 convolution_add_fusion.24
  303.3 1.5 convolution_add_fusion.23
  304.8 1.5 convolution_add_fusion.22
  306.2 1.5 convolution_add_fusion.21
  307.7 1.6 convolution_add_fusion.20
  309.3 1.5 convolution_add_fusion.19
  310.8 1.5 convolution_add_fusion.18
  312.2 1.5 convolution_add_fusion.17
  313.7 1.3 convolution_add_fusion.16
  (186 shorter events, 42.7 us)
Async XLA Ops:
  6.5 90.8 %copy-start.1 = (bf16[4,8,10,384]{3,1,2,0:T(8,128)(2,1)S(1)}, bf16[4,8,10,384]{3,1,2,0:T(8,128)(2,1)}, u32[]{:S(2)}) copy-start(bf16[4,8,10,384]{3,1,2,0:T(8,128)(2,1)} %param.7) | copy-start | bytes 737284
  6.5 91.0 %copy-start.35 = (f32[384]{0:T(512)S(1)}, f32[384]{0:T(512)}, u32[]{:S(2)}) copy-start(f32[384]{0:T(512)} %param.8) | copy-start | bytes 4612
  6.5 46.8 %all-gather.5.cloned.1.call-start = ((), (), s32[]{:S(2)}) async-start(), calls=%async_computation | async-start | bytes 2506752 | tf_op jit(solution)/shard_map/all_gather | solution.py:57
  7.3 86.4 %all-gather.9.cloned.1.call-start = ((), (), s32[]{:S(2)}) async-start(), calls=%async_computation.2 | async-start | bytes 2506752 | tf_op jit(solution)/shard_map/all_gather | solution.py:57
  8.0 168.2 %all-gather.7.cloned.1.call-start = ((), (), s32[]{:S(2)}) async-start(), calls=%async_computation.1 | async-start | bytes 9953280 | tf_op jit(solution)/shard_map/all_gather | solution.py:59
  57.1 205.1 %all-gather.11.cloned.1.call-start = ((), (), s32[]{:S(2)}) async-start(), calls=%async_computation.3 | async-start | bytes 9953280 | tf_op jit(solution)/shard_map/all_gather | solution.py:59
  97.9 7.1 %collective-permute-start = (bf16[2,8,10,384]{3,2,1,0:T(8,128)(2,1)S(1)}, bf16[2,8,10,384]{3,2,1,0:T(8,128)(2,1)S(1)}, u32[]{:S(2)}, u32[]{:S(2)}) collective-permute-start(bf16[2,8,10,384]{3,2,1,0:T(8,128)(2,1)S(1)} %slice.512), channel_id=1, source_target_pairs={{0,64},{64,128},{128,192},{1,65},{65,129},{129,193},{2,66},{66,130... | collective-permute-start | bytes 368648 | tf_op jit(solution)/shard_map/ppermute | solution.py:10
  105.0 7.0 %collective-permute-start.2 = (bf16[6,1,10,384]{3,2,1,0:T(8,128)(2,1)S(1)}, bf16[6,1,10,384]{3,2,1,0:T(8,128)(2,1)S(1)}, u32[]{:S(2)}, u32[]{:S(2)}) collective-permute-start(bf16[6,1,10,384]{3,2,1,0:T(8,128)(2,1)S(1)} %get-tuple-element.72), channel_id=1, source_target_pairs={{16,0},{32,16},{48,32},{17,1},{33,17},{49,33},{18,2},{34,18},{50,3... | collective-permute-start | bytes 138248 | tf_op jit(solution)/shard_map/ppermute | solution.py:21
  106.3 7.0 %collective-permute-start.1 = (bf16[6,1,10,384]{3,2,1,0:T(8,128)(2,1)S(1)}, bf16[6,1,10,384]{3,2,1,0:T(8,128)(2,1)S(1)}, u32[]{:S(2)}, u32[]{:S(2)}) collective-permute-start(bf16[6,1,10,384]{3,2,1,0:T(8,128)(2,1)S(1)} %get-tuple-element.71), channel_id=1, source_target_pairs={{0,16},{16,32},{32,48},{1,17},{17,33},{33,49},{2,18},{18,34},{34,5... | collective-permute-start | bytes 138248 | tf_op jit(solution)/shard_map/ppermute | solution.py:20
  114.2 12.3 %collective-permute-start.3 = (bf16[6,10,1,384]{3,2,1,0:T(2,128)(2,1)}, bf16[6,10,1,384]{3,2,1,0:T(2,128)(2,1)S(1)}, u32[]{:S(2)}, u32[]{:S(2)}) collective-permute-start(bf16[6,10,1,384]{3,2,1,0:T(2,128)(2,1)} %get-tuple-element.47), channel_id=1, source_target_pairs={{0,1},{1,2},{2,3},{3,4},{4,5},{5,6},{6,7},{7,8},{8,9},{9,10},{10,1... | collective-permute-start | bytes 138248 | tf_op jit(solution)/shard_map/ppermute | solution.py:20
  119.1 7.4 %collective-permute-start.4 = (bf16[6,10,1,384]{3,2,1,0:T(2,128)(2,1)}, bf16[6,10,1,384]{3,2,1,0:T(2,128)(2,1)S(1)}, u32[]{:S(2)}, u32[]{:S(2)}) collective-permute-start(bf16[6,10,1,384]{3,2,1,0:T(2,128)(2,1)} %get-tuple-element.48), channel_id=1, source_target_pairs={{1,0},{2,1},{3,2},{4,3},{5,4},{6,5},{7,6},{8,7},{9,8},{10,9},{11,1... | collective-permute-start | bytes 138248 | tf_op jit(solution)/shard_map/ppermute | solution.py:21
  148.1 35.8 %copy-start.7 = (bf16[320,384]{1,0:T(8,128)(2,1)S(1)}, bf16[320,384]{1,0:T(8,128)(2,1)}, u32[]{:S(2)}) copy-start(bf16[320,384]{1,0:T(8,128)(2,1)} %reshape.201) | copy-start | bytes 737284
  148.9 37.1 %copy-start.14 = (bf16[320,384]{1,0:T(8,128)(2,1)S(1)}, bf16[320,384]{1,0:T(8,128)(2,1)}, u32[]{:S(2)}) copy-start(bf16[320,384]{1,0:T(8,128)(2,1)} %reshape.204) | copy-start | bytes 737284
  151.4 36.3 %copy-start.26 = (bf16[320,384]{1,0:T(8,128)(2,1)S(1)}, bf16[320,384]{1,0:T(8,128)(2,1)}, u32[]{:S(2)}) copy-start(bf16[320,384]{1,0:T(8,128)(2,1)} %reshape.206) | copy-start | bytes 737284
  151.5 33.8 %copy-start.31 = (bf16[320,384]{1,0:T(8,128)(2,1)S(1)}, bf16[320,384]{1,0:T(8,128)(2,1)}, u32[]{:S(2)}) copy-start(bf16[320,384]{1,0:T(8,128)(2,1)} %reshape.202) | copy-start | bytes 737284
  151.5 34.2 %copy-start.29 = (bf16[320,384]{1,0:T(8,128)(2,1)S(1)}, bf16[320,384]{1,0:T(8,128)(2,1)}, u32[]{:S(2)}) copy-start(bf16[320,384]{1,0:T(8,128)(2,1)} %reshape.203) | copy-start | bytes 737284
  176.2 9.1 %copy-start = (bf16[27,384,384]{2,1,0:T(8,128)(2,1)S(1)}, bf16[27,384,384]{2,1,0:T(8,128)(2,1)}, u32[]{:S(2)}) copy-start(bf16[27,384,384]{2,1,0:T(8,128)(2,1)} %all-gather.7.cloned.1.call-done) | copy-start | bytes 23887876
  176.2 11.9 %copy-start.12 = (bf16[320,384]{1,0:T(8,128)(2,1)S(1)}, bf16[320,384]{1,0:T(8,128)(2,1)}, u32[]{:S(2)}) copy-start(bf16[320,384]{1,0:T(8,128)(2,1)} %reshape.207) | copy-start | bytes 737284
  177.8 10.7 %copy-start.25 = (bf16[320,384]{1,0:T(8,128)(2,1)S(1)}, bf16[320,384]{1,0:T(8,128)(2,1)}, u32[]{:S(2)}) copy-start(bf16[320,384]{1,0:T(8,128)(2,1)} %reshape.208) | copy-start | bytes 737284
  181.0 7.8 %copy-start.23 = (bf16[320,384]{1,0:T(8,128)(2,1)S(1)}, bf16[320,384]{1,0:T(8,128)(2,1)}, u32[]{:S(2)}) copy-start(bf16[320,384]{1,0:T(8,128)(2,1)} %reshape.209) | copy-start | bytes 737284
  182.4 6.7 %copy-start.33 = (bf16[320,384]{1,0:T(8,128)(2,1)S(1)}, bf16[320,384]{1,0:T(8,128)(2,1)}, u32[]{:S(2)}) copy-start(bf16[320,384]{1,0:T(8,128)(2,1)} %reshape.210) | copy-start | bytes 737284
  183.9 5.6 %copy-start.20 = (bf16[320,384]{1,0:T(8,128)(2,1)S(1)}, bf16[320,384]{1,0:T(8,128)(2,1)}, u32[]{:S(2)}) copy-start(bf16[320,384]{1,0:T(8,128)(2,1)} %reshape.212) | copy-start | bytes 737284
  185.3 4.5 %copy-start.10 = (bf16[320,384]{1,0:T(8,128)(2,1)S(1)}, bf16[320,384]{1,0:T(8,128)(2,1)}, u32[]{:S(2)}) copy-start(bf16[320,384]{1,0:T(8,128)(2,1)} %reshape.213) | copy-start | bytes 737284
  185.7 4.5 %copy-start.18 = (bf16[320,384]{1,0:T(8,128)(2,1)S(1)}, bf16[320,384]{1,0:T(8,128)(2,1)}, u32[]{:S(2)}) copy-start(bf16[320,384]{1,0:T(8,128)(2,1)} %reshape.214) | copy-start | bytes 737284
  186.0 4.5 %copy-start.17 = (bf16[320,384]{1,0:T(8,128)(2,1)S(1)}, bf16[320,384]{1,0:T(8,128)(2,1)}, u32[]{:S(2)}) copy-start(bf16[320,384]{1,0:T(8,128)(2,1)} %reshape.215) | copy-start | bytes 737284
  186.4 4.5 %copy-start.8 = (bf16[320,384]{1,0:T(8,128)(2,1)S(1)}, bf16[320,384]{1,0:T(8,128)(2,1)}, u32[]{:S(2)}) copy-start(bf16[320,384]{1,0:T(8,128)(2,1)} %reshape.216) | copy-start | bytes 737284
  187.7 3.5 %copy-start.16 = (bf16[320,384]{1,0:T(8,128)(2,1)S(1)}, bf16[320,384]{1,0:T(8,128)(2,1)}, u32[]{:S(2)}) copy-start(bf16[320,384]{1,0:T(8,128)(2,1)} %reshape.217) | copy-start | bytes 737284
  188.1 3.5 %copy-start.15 = (bf16[320,384]{1,0:T(8,128)(2,1)S(1)}, bf16[320,384]{1,0:T(8,128)(2,1)}, u32[]{:S(2)}) copy-start(bf16[320,384]{1,0:T(8,128)(2,1)} %reshape.218) | copy-start | bytes 737284
  188.4 3.5 %copy-start.4 = (bf16[320,384]{1,0:T(8,128)(2,1)S(1)}, bf16[320,384]{1,0:T(8,128)(2,1)}, u32[]{:S(2)}) copy-start(bf16[320,384]{1,0:T(8,128)(2,1)} %reshape.219) | copy-start | bytes 737284
  189.5 3.5 %copy-start.5 = (bf16[320,384]{1,0:T(8,128)(2,1)S(1)}, bf16[320,384]{1,0:T(8,128)(2,1)}, u32[]{:S(2)}) copy-start(bf16[320,384]{1,0:T(8,128)(2,1)} %reshape.222) | copy-start | bytes 737284
  189.9 3.5 %copy-start.34 = (f32[384]{0:T(512)S(1)}, f32[384]{0:T(512)}, u32[]{:S(2)}) copy-start(f32[384]{0:T(512)} %param.10) | copy-start | bytes 4612
  190.2 3.8 %copy-start.36 = (f32[384]{0:T(512)S(1)}, f32[384]{0:T(512)}, u32[]{:S(2)}) copy-start(f32[384]{0:T(512)} %param.11) | copy-start | bytes 4612
  194.3 6.8 %collective-permute-start.5 = (bf16[2,8,10,384]{3,2,1,0:T(8,128)(2,1)S(1)}, bf16[2,8,10,384]{3,2,1,0:T(8,128)(2,1)S(1)}, u32[]{:S(2)}, u32[]{:S(2)}) collective-permute-start(bf16[2,8,10,384]{3,2,1,0:T(8,128)(2,1)S(1)} %slice.566), channel_id=1, source_target_pairs={{0,64},{64,128},{128,192},{1,65},{65,129},{129,193},{2,66},{66,130... | collective-permute-start | bytes 368648 | tf_op jit(solution)/shard_map/ppermute | solution.py:10
  201.2 7.2 %collective-permute-start.7 = (bf16[6,1,10,384]{3,2,1,0:T(8,128)(2,1)S(1)}, bf16[6,1,10,384]{3,2,1,0:T(8,128)(2,1)S(1)}, u32[]{:S(2)}, u32[]{:S(2)}) collective-permute-start(bf16[6,1,10,384]{3,2,1,0:T(8,128)(2,1)S(1)} %get-tuple-element.66), channel_id=1, source_target_pairs={{16,0},{32,16},{48,32},{17,1},{33,17},{49,33},{18,2},{34,18},{50,3... | collective-permute-start | bytes 138248 | tf_op jit(solution)/shard_map/ppermute | solution.py:21
  202.5 6.8 %collective-permute-start.6 = (bf16[6,1,10,384]{3,2,1,0:T(8,128)(2,1)S(1)}, bf16[6,1,10,384]{3,2,1,0:T(8,128)(2,1)S(1)}, u32[]{:S(2)}, u32[]{:S(2)}) collective-permute-start(bf16[6,1,10,384]{3,2,1,0:T(8,128)(2,1)S(1)} %get-tuple-element.65), channel_id=1, source_target_pairs={{0,16},{16,32},{32,48},{1,17},{17,33},{33,49},{2,18},{18,34},{34,5... | collective-permute-start | bytes 138248 | tf_op jit(solution)/shard_map/ppermute | solution.py:20
  210.1 60.4 %collective-permute-start.8 = (bf16[6,10,1,384]{3,2,1,0:T(2,128)(2,1)}, bf16[6,10,1,384]{3,2,1,0:T(2,128)(2,1)}, u32[]{:S(2)}, u32[]{:S(2)}) collective-permute-start(bf16[6,10,1,384]{3,2,1,0:T(2,128)(2,1)} %get-tuple-element.25), channel_id=1, source_target_pairs={{0,1},{1,2},{2,3},{3,4},{4,5},{5,6},{6,7},{7,8},{8,9},{9,10},{10,1... | collective-permute-start | bytes 138248 | tf_op jit(solution)/shard_map/ppermute | solution.py:20
  215.9 54.6 %collective-permute-start.9 = (bf16[6,10,1,384]{3,2,1,0:T(2,128)(2,1)}, bf16[6,10,1,384]{3,2,1,0:T(2,128)(2,1)}, u32[]{:S(2)}, u32[]{:S(2)}) collective-permute-start(bf16[6,10,1,384]{3,2,1,0:T(2,128)(2,1)} %get-tuple-element.26), channel_id=1, source_target_pairs={{1,0},{2,1},{3,2},{4,3},{5,4},{6,5},{7,6},{8,7},{9,8},{10,9},{11,1... | collective-permute-start | bytes 138248 | tf_op jit(solution)/shard_map/ppermute | solution.py:21
  277.6 22.3 %copy-start.3 = (bf16[4,8,10,384]{3,2,1,0:T(8,128)(2,1)S(1)}, bf16[4,8,10,384]{3,2,1,0:T(8,128)(2,1)}, u32[]{:S(2)}) copy-start(bf16[4,8,10,384]{3,2,1,0:T(8,128)(2,1)} %get-tuple-element.15) | copy-start | bytes 737284
  277.6 22.5 %copy-start.2 = (bf16[4,8,10,384]{3,2,1,0:T(8,128)(2,1)S(1)}, bf16[4,8,10,384]{3,2,1,0:T(8,128)(2,1)}, u32[]{:S(2)}) copy-start(bf16[4,8,10,384]{3,2,1,0:T(8,128)(2,1)} %get-tuple-element.14) | copy-start | bytes 737284
  299.9 13.8 %copy-start.30 = (bf16[320,384]{1,0:T(8,128)(2,1)S(1)}, bf16[320,384]{1,0:T(8,128)(2,1)}, u32[]{:S(2)}) copy-start(bf16[320,384]{1,0:T(8,128)(2,1)} %reshape.234) | copy-start | bytes 737284
  300.1 15.0 %copy-start.13 = (bf16[320,384]{1,0:T(8,128)(2,1)S(1)}, bf16[320,384]{1,0:T(8,128)(2,1)}, u32[]{:S(2)}) copy-start(bf16[320,384]{1,0:T(8,128)(2,1)} %reshape.235) | copy-start | bytes 737284
  300.3 16.1 %slice-start = ((s8[7962624]{0:T(1024)(128)(4,1)}), s8[4194304]{0:T(1024)(128)(4,1)S(1)}, s32[]{:S(2)}) async-start(s8[7962624]{0:T(1024)(128)(4,1)} %bitcast.217), calls=%async_computation.4 | async-start | bytes 8388608
  300.3 16.1 %copy-start.28 = (bf16[320,384]{1,0:T(8,128)(2,1)S(1)}, bf16[320,384]{1,0:T(8,128)(2,1)}, u32[]{:S(2)}) copy-start(bf16[320,384]{1,0:T(8,128)(2,1)} %reshape.236) | copy-start | bytes 737284
  303.3 13.4 %copy-start.27 = (bf16[320,384]{1,0:T(8,128)(2,1)S(1)}, bf16[320,384]{1,0:T(8,128)(2,1)}, u32[]{:S(2)}) copy-start(bf16[320,384]{1,0:T(8,128)(2,1)} %reshape.237) | copy-start | bytes 737284
  304.8 12.3 %copy-start.32 = (bf16[320,384]{1,0:T(8,128)(2,1)S(1)}, bf16[320,384]{1,0:T(8,128)(2,1)}, u32[]{:S(2)}) copy-start(bf16[320,384]{1,0:T(8,128)(2,1)} %reshape.238) | copy-start | bytes 737284
  306.2 11.2 %copy-start.24 = (bf16[320,384]{1,0:T(8,128)(2,1)S(1)}, bf16[320,384]{1,0:T(8,128)(2,1)}, u32[]{:S(2)}) copy-start(bf16[320,384]{1,0:T(8,128)(2,1)} %reshape.240) | copy-start | bytes 737284
  307.7 8.7 %slice-start.1 = ((s8[7962624]{0:T(1024)(128)(4,1)}), s8[3768320]{0:T(1024)(128)(4,1)S(1)}, s32[]{:S(2)}) async-start(s8[7962624]{0:T(1024)(128)(4,1)} %bitcast.217), calls=%async_computation.5 | async-start | bytes 7536640
  307.7 10.1 %copy-start.11 = (bf16[320,384]{1,0:T(8,128)(2,1)S(1)}, bf16[320,384]{1,0:T(8,128)(2,1)}, u32[]{:S(2)}) copy-start(bf16[320,384]{1,0:T(8,128)(2,1)} %reshape.241) | copy-start | bytes 737284
  309.3 8.9 %copy-start.22 = (bf16[320,384]{1,0:T(8,128)(2,1)S(1)}, bf16[320,384]{1,0:T(8,128)(2,1)}, u32[]{:S(2)}) copy-start(bf16[320,384]{1,0:T(8,128)(2,1)} %reshape.242) | copy-start | bytes 737284
  310.8 7.7 %copy-start.21 = (bf16[320,384]{1,0:T(8,128)(2,1)S(1)}, bf16[320,384]{1,0:T(8,128)(2,1)}, u32[]{:S(2)}) copy-start(bf16[320,384]{1,0:T(8,128)(2,1)} %reshape.243) | copy-start | bytes 737284
  312.2 6.6 %copy-start.9 = (bf16[320,384]{1,0:T(8,128)(2,1)S(1)}, bf16[320,384]{1,0:T(8,128)(2,1)}, u32[]{:S(2)}) copy-start(bf16[320,384]{1,0:T(8,128)(2,1)} %reshape.244) | copy-start | bytes 737284
  313.7 5.5 %copy-start.19 = (bf16[320,384]{1,0:T(8,128)(2,1)S(1)}, bf16[320,384]{1,0:T(8,128)(2,1)}, u32[]{:S(2)}) copy-start(bf16[320,384]{1,0:T(8,128)(2,1)} %reshape.245) | copy-start | bytes 737284
  317.8 3.3 copy-start.6
  318.5 3.3 %copy-start.37 = (f32[384]{0:T(512)S(1)}, f32[384]{0:T(512)}, u32[]{:S(2)}) copy-start(f32[384]{0:T(512)} %param.13) | copy-start | bytes 4612
Sparse Core Ops, SparseCore 0:
  9.2 44.1 all-gather.4
  55.2 38.3 all-gather.8
  95.4 80.7 all-gather.6
  177.9 84.2 all-gather.10
where the time goes:
time: 331 us; the launch traced here: 329 us
  waiting for transfers between devices  159 us (48%)
  local copies, waits for them, and re-layouts  79.1 us (24%)
  matrix products  39.5 us (12%)
  starting transfers between devices  32 us (10%)
  between operations  14.3 us (4%)
  other arithmetic  5.48 us (2%)
    all_gather x2, waiting for transfers between devices, convolve(): row_kernel = lax.all_gather(kernel, 'width', axis=1, tiled=True)  81.8 us
    all_gather x2, waiting for transfers between devices, convolve(): lax.all_gather(row_kernel, 'height', axis=1, tiled=True)  66.6 us
    reshape x53, local copies, waits for them, and re-layouts, fold_piece(): window.reshape(-1, count_in)  63 us
    dot_general x54, matrix products, fold_piece(): jnp.dot(window.reshape(-1, count_in), piece[9 * step_t + 3 * step_h + ste...  39.5 us
    ppermute x4, starting transfers between devices, extended(): before = lax.ppermute(last, axis, up)  18.9 us
    slice x6, local copies, waits for them, and re-layouts, fold_piece(): widened[step_t:step_t + frames, step_h:step_h + rows, step_w:step_w + cols]  7.5 us
    all_gather x2, local copies, waits for them, and re-layouts, convolve(): row_kernel = lax.all_gather(kernel, 'width', axis=1, tiled=True)  7.38 us
    ppermute x2, waiting for transfers between devices, passed_along(): return lax.ppermute(x, axis, pairs)  6.76 us
  transfers between devices with their start and end apart: 14, of which 8 were waited for; matrix products, arithmetic and copies ran while one was open for 22% of the time, Pallas kernels for 0%

commit v1 on v0

--- a/solution.py
+++ b/solution.py
@@ -56,7 +56,12 @@
     fold_piece = make_folder(widened, frames, rows, cols)
     row_kernel = lax.all_gather(kernel, "width", axis=1, tiled=True)
     total = fold_piece(
-        empty, lax.all_gather(row_kernel, "height", axis=1, tiled=True), jnp.int32(0)
+        empty,
+        jnp.concatenate(
+            lax.all_to_all(jnp.stack([row_kernel] * lax.axis_size("height")), "height", 0, 0),
+            axis=1,
+        ),
+        jnp.int32(0),
     )
     return total.reshape(frames, rows, cols, out_chans) + bias
 

time: 331 us -> 378 us (1.14)
  waiting for transfers between devices: 159 us -> 191 us
  local copies, waits for them, and re-layouts: 79.1 us -> 103 us
  matrix products: 39.5 us -> 20.1 us
  starting transfers between devices: 32 us -> 40.5 us
    ppermute x4, waiting for transfers between devices: 0.01 us -> 73.7 us  [extended(): after = lax.ppermute(first, axis, down)]
    all_gather x2 -> x0, waiting for transfers between devices: 66.6 us -> none  [convolve(): lax.all_gather(row_kernel, 'height', axis=1, tiled=True)]
    all_to_all x0 -> x2, waiting for transfers between devices: none -> 66.3 us  [convolve(): lax.all_to_all(jnp.stack([row_kernel] * lax.axis_size('height')), 'height...]
    all_gather x2, waiting for transfers between devices: 81.8 us -> 46.1 us  [convolve(): row_kernel = lax.all_gather(kernel, 'width', axis=1, tiled=True)]
    dot_general x54, matrix products: 39.5 us -> 20.1 us  [fold_piece(): jnp.dot(window.reshape(-1, count_in), piece[9 * step_t + 3 * step_h + ste...]
    slice x0 -> x4, local copies, waits for them, and re-layouts: none -> 13.5 us  [fold_piece(): piece[9 * step_t + 3 * step_h + step_w]]
    all_to_all x0 -> x2, starting transfers between devices: none -> 11.4 us  [convolve(): lax.all_to_all(jnp.stack([row_kernel] * lax.axis_size('height')), 'height...]
    unnamed x80 -> x168, local copies, waits for them, and re-layouts: 0.17 us -> 8.17 us
  transfers between devices with their start and end apart: 14 -> 14, of which waited for: 8 -> 5; matrix products, arithmetic and copies ran while one was open for 22% -> 18% of each run, Pallas kernels for 0% -> 0%
where the time goes in v1:
time: 378 us; the launch traced here: 375 us
  waiting for transfers between devices  191 us (51%)
  local copies, waits for them, and re-layouts  103 us (27%)
  starting transfers between devices  40.5 us (11%)
  matrix products  20.1 us (5%)
  between operations  14.4 us (4%)
  other arithmetic  6.38 us (2%)
    ppermute x4, waiting for transfers between devices, extended(): after = lax.ppermute(first, axis, down)  73.7 us
    all_to_all x2, waiting for transfers between devices, convolve(): lax.all_to_all(jnp.stack([row_kernel] * lax.axis_size('height')), 'height...  66.3 us
    reshape x53, local copies, waits for them, and re-layouts, fold_piece(): window.reshape(-1, count_in)  60.4 us
    all_gather x2, waiting for transfers between devices, convolve(): row_kernel = lax.all_gather(kernel, 'width', axis=1, tiled=True)  46.1 us
    dot_general x54, matrix products, fold_piece(): jnp.dot(window.reshape(-1, count_in), piece[9 * step_t + 3 * step_h + ste...  20.1 us
    ppermute x4, starting transfers between devices, extended(): before = lax.ppermute(last, axis, up)  16.2 us
    slice x4, local copies, waits for them, and re-layouts, fold_piece(): piece[9 * step_t + 3 * step_h + step_w]  13.5 us
    all_to_all x2, starting transfers between devices, convolve(): lax.all_to_all(jnp.stack([row_kernel] * lax.axis_size('height')), 'height...  11.4 us
  transfers between devices with their start and end apart: 14, of which 5 were waited for; matrix products, arithmetic and copies ran while one was open for 18% of the time, Pallas kernels for 0%

profile of v1, /device:TPU:1, one launch (start us, length us, event | category | flops | bytes accessed | tf_op | source)
XLA Modules:
  0.0 375.3 jit_solution(7004110574929730363)
XLA Ops:
  7.3 46.1 %all-gather.3.cloned.1.call-done = bf16[27,96,384]{2,0,1:T(8,128)(2,1)} async-done(((bf16[27,6,384]{2,0,1:T(8,128)(2,1)}), bf16[27,96,384]{2,0,1:T(8,128)(2,1)}) %all-gather.3.cloned.1.call-update) | async-done | bytes 1990672 | tf_op jit(solution)/shard_map/all_gather | solution.py:57
  53.4 2.4 copy.17
  55.7 3.8 %stack.4 = bf16[4,27,96,384]{3,2,1,0:T(8,128)(2,1)} broadcast(bf16[27,96,384]{2,1,0:T(8,128)(2,1)S(1)} %copy.17), dimensions={1,2,3} | broadcast | bytes 9953280 | tf_op jit(solution)/shard_map/stack | solution.py:61
  59.6 5.7 %all-to-all-start = ((bf16[4,27,96,384]{3,2,1,0:T(8,128)(2,1)}), bf16[4,27,96,384]{3,2,1,0:T(8,128)(2,1)}, u32[]{:S(2)}, u32[]{:S(2)}) async-start(bf16[4,27,96,384]{3,2,1,0:T(8,128)(2,1)} %stack.4), calls=%async_computation | async-start | bytes 15925248 | tf_op jit(solution)/shard_map/all_to_all | solution.py:61
  66.6 3.1 collective-permute-start
  69.7 0.8 reshape.340
  70.5 3.2 collective-permute-done
  73.7 1.3 collective-permute-start.2
  75.0 4.0 %collective-permute-start.1 = (bf16[6,1,10,384]{3,2,1,0:T(8,128)(2,1)S(1)}, bf16[6,1,10,384]{3,2,1,0:T(8,128)(2,1)S(1)}, u32[]{:S(2)}, u32[]{:S(2)}) collective-permute-start(bf16[6,1,10,384]{3,2,1,0:T(8,128)(2,1)S(1)} %get-tuple-element.125), channel_id=1, source_target_pairs={{0,16},{16,32},{32,48},{1,17},{17,33},{33,49},{2,18},{18,34},{34,5... | collective-permute-start | bytes 138248 | tf_op jit(solution)/shard_map/ppermute | solution.py:20
  79.2 0.8 reshape.322
  80.7 73.7 %collective-permute-done.2 = bf16[6,1,10,384]{3,2,1,0:T(8,128)(2,1)S(1)} collective-permute-done((bf16[6,1,10,384]{3,2,1,0:T(8,128)(2,1)S(1)}, bf16[6,1,10,384]{3,2,1,0:T(8,128)(2,1)S(1)}, u32[]{:S(2)}, u32[]{:S(2)}) %collective-permute-start.2) | collective-permute-done | bytes 46112 | tf_op jit(solution)/shard_map/ppermute | solution.py:21
  154.5 0.8 pad_maximum_fusion.13
  155.3 3.7 collective-permute-start.3
  159.0 1.9 collective-permute-start.4
  161.4 0.8 reshape.319
  162.2 0.8 reshape.325
  163.0 0.8 reshape.328
  166.2 1.5 maximum_maximum_fusion
  167.7 2.2 fusion.32
  169.9 1.8 reshape.332
  171.7 1.8 reshape.317
  173.4 1.8 reshape.320
  175.2 1.8 reshape.321
  177.0 1.8 reshape.323
  178.8 1.8 reshape.324
  180.5 1.8 reshape.326
  182.3 1.8 reshape.327
  184.1 1.8 reshape.329
  185.9 1.8 reshape.330
  188.5 0.8 reshape.335
  190.6 2.4 copy.18
  193.0 3.9 %stack.5 = bf16[4,27,96,384]{3,2,1,0:T(8,128)(2,1)} broadcast(bf16[27,96,384]{2,1,0:T(8,128)(2,1)S(1)} %copy.18), dimensions={1,2,3} | broadcast | bytes 9953280 | tf_op jit(solution)/shard_map/stack | solution.py:61
  196.8 5.7 %all-to-all-start.1 = ((bf16[4,27,96,384]{3,2,1,0:T(8,128)(2,1)}), bf16[4,27,96,384]{3,2,1,0:T(8,128)(2,1)}, u32[]{:S(2)}, u32[]{:S(2)}) async-start(bf16[4,27,96,384]{3,2,1,0:T(8,128)(2,1)} %stack.5), calls=%async_computation.1 | async-start | bytes 15925248 | tf_op jit(solution)/shard_map/all_to_all | solution.py:61
  202.5 3.4 fusion.28
  206.0 1.9 fusion.29
  221.0 3.1 collective-permute-start.5
  224.1 66.3 %all-to-all-done.1 = bf16[4,27,96,384]{3,2,1,0:T(8,128)(2,1)} async-done(((bf16[4,27,96,384]{3,2,1,0:T(8,128)(2,1)}), bf16[4,27,96,384]{3,2,1,0:T(8,128)(2,1)}, u32[]{:S(2)}, u32[]{:S(2)}) %all-to-all-start.1) | async-done | bytes 7962656 | tf_op jit(solution)/shard_map/all_to_all | solution.py:61
  290.4 5.1 %fusion.26 = (bf16[1,4,96,384]{3,2,0,1:T(8,128)(2,1)}, bf16[1,4,96,384]{3,2,0,1:T(8,128)(2,1)}, bf16[1,4,96,384]{3,2,0,1:T(8,128)(2,1)}, bf16[1,4,96,384]{3,2,0,...) fusion(bf16[27,4,96,384]{3,2,0,1:T(8,128)(2,1)} %bitcast.28), kind=kLoop, calls=%fused_computation.111 | loop fusion | bytes 11206656 | tf_op jit(solution)/shard_map/slice | solution.py:45
  295.5 3.0 fusion.27
  298.6 1.3 collective-permute-start.7
  299.9 4.0 %collective-permute-start.6 = (bf16[6,1,10,384]{3,2,1,0:T(8,128)(2,1)S(1)}, bf16[6,1,10,384]{3,2,1,0:T(8,128)(2,1)S(1)}, u32[]{:S(2)}, u32[]{:S(2)}) collective-permute-start(bf16[6,1,10,384]{3,2,1,0:T(8,128)(2,1)S(1)} %get-tuple-element.119), channel_id=1, source_target_pairs={{0,16},{16,32},{32,48},{1,17},{17,33},{33,49},{2,18},{18,34},{34,5... | collective-permute-start | bytes 138248 | tf_op jit(solution)/shard_map/ppermute | solution.py:20
  305.9 0.8 pad_maximum_fusion.9
  306.7 4.5 %collective-permute-start.8 = (bf16[6,10,1,384]{3,2,1,0:T(2,128)(2,1)}, bf16[6,10,1,384]{3,2,1,0:T(2,128)(2,1)}, u32[]{:S(2)}, u32[]{:S(2)}) collective-permute-start(bf16[6,10,1,384]{3,2,1,0:T(2,128)(2,1)} %get-tuple-element.79), channel_id=1, source_target_pairs={{0,1},{1,2},{2,3},{3,4},{4,5},{5,6},{6,7},{7,8},{8,9},{9,10},{10,1... | collective-permute-start | bytes 138248 | tf_op jit(solution)/shard_map/ppermute | solution.py:20
  311.3 2.1 collective-permute-start.9
  314.6 1.1 fusion.34
  316.3 1.8 reshape.354
  318.1 0.8 reshape.357
  318.9 1.8 reshape.363
  322.3 1.6 maximum_maximum_fusion.1
  323.8 1.8 fusion.30
  325.6 1.8 reshape.361
  327.4 1.8 fusion.31
  329.2 1.8 reshape.346
  331.1 1.8 reshape.349
  332.9 1.8 reshape.350
  335.5 1.8 reshape.353
  337.3 1.8 reshape.355
  339.1 1.8 reshape.356
  341.7 1.8 reshape.359
  343.5 1.8 reshape.362
  346.0 1.8 reshape.365
  347.9 0.8 reshape.367
  351.8 1.3 fusion.41
  353.1 1.3 convolution_add_fusion.24
  (277 shorter events, 45.0 us)
Async XLA Ops:
  6.5 46.8 %all-gather.3.cloned.1.call-start = ((), (), s32[]{:S(2)}) async-start(), calls=%async_computation.2 | async-start | bytes 2506752 | tf_op jit(solution)/shard_map/all_gather | solution.py:57
  59.6 6.4 %copy-start = (bf16[4,8,10,384]{3,1,2,0:T(8,128)(2,1)S(1)}, bf16[4,8,10,384]{3,1,2,0:T(8,128)(2,1)}, u32[]{:S(2)}) copy-start(bf16[4,8,10,384]{3,1,2,0:T(8,128)(2,1)} %param.7) | copy-start | bytes 737284
  59.6 6.6 %copy-start.81 = (f32[384]{0:T(512)S(1)}, f32[384]{0:T(512)}, u32[]{:S(2)}) copy-start(f32[384]{0:T(512)} %param.8) | copy-start | bytes 4612
  59.6 133.4 %all-to-all-start = ((bf16[4,27,96,384]{3,2,1,0:T(8,128)(2,1)}), bf16[4,27,96,384]{3,2,1,0:T(8,128)(2,1)}, u32[]{:S(2)}, u32[]{:S(2)}) async-start(bf16[4,27,96,384]{3,2,1,0:T(8,128)(2,1)} %stack.4), calls=%async_computation | async-start | bytes 15925248 | tf_op jit(solution)/shard_map/all_to_all | solution.py:61
  65.3 125.3 %all-gather.5.cloned.1.call-start = ((), (), s32[]{:S(2)}) async-start(), calls=%async_computation.3 | async-start | bytes 2506752 | tf_op jit(solution)/shard_map/all_gather | solution.py:57
  66.6 7.1 %collective-permute-start = (bf16[2,8,10,384]{3,2,1,0:T(8,128)(2,1)S(1)}, bf16[2,8,10,384]{3,2,1,0:T(8,128)(2,1)S(1)}, u32[]{:S(2)}, u32[]{:S(2)}) collective-permute-start(bf16[2,8,10,384]{3,2,1,0:T(8,128)(2,1)S(1)} %slice.566), channel_id=1, source_target_pairs={{0,64},{64,128},{128,192},{1,65},{65,129},{129,193},{2,66},{66,130... | collective-permute-start | bytes 368648 | tf_op jit(solution)/shard_map/ppermute | solution.py:10
  73.7 80.7 %collective-permute-start.2 = (bf16[6,1,10,384]{3,2,1,0:T(8,128)(2,1)S(1)}, bf16[6,1,10,384]{3,2,1,0:T(8,128)(2,1)S(1)}, u32[]{:S(2)}, u32[]{:S(2)}) collective-permute-start(bf16[6,1,10,384]{3,2,1,0:T(8,128)(2,1)S(1)} %get-tuple-element.126), channel_id=1, source_target_pairs={{16,0},{32,16},{48,32},{17,1},{33,17},{49,33},{18,2},{34,18},{50,3... | collective-permute-start | bytes 138248 | tf_op jit(solution)/shard_map/ppermute | solution.py:21
  75.0 79.4 %collective-permute-start.1 = (bf16[6,1,10,384]{3,2,1,0:T(8,128)(2,1)S(1)}, bf16[6,1,10,384]{3,2,1,0:T(8,128)(2,1)S(1)}, u32[]{:S(2)}, u32[]{:S(2)}) collective-permute-start(bf16[6,1,10,384]{3,2,1,0:T(8,128)(2,1)S(1)} %get-tuple-element.125), channel_id=1, source_target_pairs={{0,16},{16,32},{32,48},{1,17},{17,33},{33,49},{2,18},{18,34},{34,5... | collective-permute-start | bytes 138248 | tf_op jit(solution)/shard_map/ppermute | solution.py:20
  155.3 10.9 %collective-permute-start.3 = (bf16[6,10,1,384]{3,2,1,0:T(2,128)(2,1)}, bf16[6,10,1,384]{3,2,1,0:T(2,128)(2,1)S(1)}, u32[]{:S(2)}, u32[]{:S(2)}) collective-permute-start(bf16[6,10,1,384]{3,2,1,0:T(2,128)(2,1)} %get-tuple-element.101), channel_id=1, source_target_pairs={{0,1},{1,2},{2,3},{3,4},{4,5},{5,6},{6,7},{7,8},{8,9},{9,10},{10,1... | collective-permute-start | bytes 138248 | tf_op jit(solution)/shard_map/ppermute | solution.py:20
  159.0 7.1 %collective-permute-start.4 = (bf16[6,10,1,384]{3,2,1,0:T(2,128)(2,1)}, bf16[6,10,1,384]{3,2,1,0:T(2,128)(2,1)}, u32[]{:S(2)}, u32[]{:S(2)}) collective-permute-start(bf16[6,10,1,384]{3,2,1,0:T(2,128)(2,1)} %get-tuple-element.102), channel_id=1, source_target_pairs={{1,0},{2,1},{3,2},{4,3},{5,4},{6,5},{7,6},{8,7},{9,8},{10,9},{11,1... | collective-permute-start | bytes 138248 | tf_op jit(solution)/shard_map/ppermute | solution.py:21
  196.8 93.6 %all-to-all-start.1 = ((bf16[4,27,96,384]{3,2,1,0:T(8,128)(2,1)}), bf16[4,27,96,384]{3,2,1,0:T(8,128)(2,1)}, u32[]{:S(2)}, u32[]{:S(2)}) async-start(bf16[4,27,96,384]{3,2,1,0:T(8,128)(2,1)} %stack.5), calls=%async_computation.1 | async-start | bytes 15925248 | tf_op jit(solution)/shard_map/all_to_all | solution.py:61
  206.0 2.0 copy-start.74
  206.0 2.3 copy-start.62
  210.6 1.0 copy-start.40
  221.0 77.6 %collective-permute-start.5 = (bf16[2,8,10,384]{3,2,1,0:T(8,128)(2,1)S(1)}, bf16[2,8,10,384]{3,2,1,0:T(8,128)(2,1)S(1)}, u32[]{:S(2)}, u32[]{:S(2)}) collective-permute-start(bf16[2,8,10,384]{3,2,1,0:T(8,128)(2,1)S(1)} %slice.620), channel_id=1, source_target_pairs={{0,64},{64,128},{128,192},{1,65},{65,129},{129,193},{2,66},{66,130... | collective-permute-start | bytes 368648 | tf_op jit(solution)/shard_map/ppermute | solution.py:10
  298.6 7.0 %collective-permute-start.7 = (bf16[6,1,10,384]{3,2,1,0:T(8,128)(2,1)S(1)}, bf16[6,1,10,384]{3,2,1,0:T(8,128)(2,1)S(1)}, u32[]{:S(2)}, u32[]{:S(2)}) collective-permute-start(bf16[6,1,10,384]{3,2,1,0:T(8,128)(2,1)S(1)} %get-tuple-element.120), channel_id=1, source_target_pairs={{16,0},{32,16},{48,32},{17,1},{33,17},{49,33},{18,2},{34,18},{50,3... | collective-permute-start | bytes 138248 | tf_op jit(solution)/shard_map/ppermute | solution.py:21
  299.9 6.0 %collective-permute-start.6 = (bf16[6,1,10,384]{3,2,1,0:T(8,128)(2,1)S(1)}, bf16[6,1,10,384]{3,2,1,0:T(8,128)(2,1)S(1)}, u32[]{:S(2)}, u32[]{:S(2)}) collective-permute-start(bf16[6,1,10,384]{3,2,1,0:T(8,128)(2,1)S(1)} %get-tuple-element.119), channel_id=1, source_target_pairs={{0,16},{16,32},{32,48},{1,17},{17,33},{33,49},{2,18},{18,34},{34,5... | collective-permute-start | bytes 138248 | tf_op jit(solution)/shard_map/ppermute | solution.py:20
  306.7 15.5 %collective-permute-start.8 = (bf16[6,10,1,384]{3,2,1,0:T(2,128)(2,1)}, bf16[6,10,1,384]{3,2,1,0:T(2,128)(2,1)}, u32[]{:S(2)}, u32[]{:S(2)}) collective-permute-start(bf16[6,10,1,384]{3,2,1,0:T(2,128)(2,1)} %get-tuple-element.79), channel_id=1, source_target_pairs={{0,1},{1,2},{2,3},{3,4},{4,5},{5,6},{6,7},{7,8},{8,9},{9,10},{10,1... | collective-permute-start | bytes 138248 | tf_op jit(solution)/shard_map/ppermute | solution.py:20
  311.3 11.0 %collective-permute-start.9 = (bf16[6,10,1,384]{3,2,1,0:T(2,128)(2,1)}, bf16[6,10,1,384]{3,2,1,0:T(2,128)(2,1)}, u32[]{:S(2)}, u32[]{:S(2)}) collective-permute-start(bf16[6,10,1,384]{3,2,1,0:T(2,128)(2,1)} %get-tuple-element.80), channel_id=1, source_target_pairs={{1,0},{2,1},{3,2},{4,3},{5,4},{6,5},{7,6},{8,7},{9,8},{10,9},{11,1... | collective-permute-start | bytes 138248 | tf_op jit(solution)/shard_map/ppermute | solution.py:21
  314.6 1.1 copy-start.32
  314.6 1.4 copy-start.76
  316.3 5.2 %copy-start.6 = (bf16[4,8,10,384]{3,2,1,0:T(8,128)(2,1)S(1)}, bf16[4,8,10,384]{3,2,1,0:T(8,128)(2,1)}, u32[]{:S(2)}) copy-start(bf16[4,8,10,384]{3,2,1,0:T(8,128)(2,1)} %get-tuple-element.103) | copy-start | bytes 737284
  329.2 5.5 %copy-start.5 = (bf16[4,8,10,384]{3,2,1,0:T(8,128)(2,1)S(1)}, bf16[4,8,10,384]{3,2,1,0:T(8,128)(2,1)}, u32[]{:S(2)}) copy-start(bf16[4,8,10,384]{3,2,1,0:T(8,128)(2,1)} %get-tuple-element.66) | copy-start | bytes 737284
  332.9 8.0 %copy-start.2 = (bf16[4,8,10,384]{3,2,1,0:T(8,128)(2,1)S(1)}, bf16[4,8,10,384]{3,2,1,0:T(8,128)(2,1)}, u32[]{:S(2)}) copy-start(bf16[4,8,10,384]{3,2,1,0:T(8,128)(2,1)} %get-tuple-element.64) | copy-start | bytes 737284
  337.3 8.0 %copy-start.1 = (bf16[4,8,10,384]{3,2,1,0:T(8,128)(2,1)S(1)}, bf16[4,8,10,384]{3,2,1,0:T(8,128)(2,1)}, u32[]{:S(2)}) copy-start(bf16[4,8,10,384]{3,2,1,0:T(8,128)(2,1)} %get-tuple-element.62) | copy-start | bytes 737284
  345.3 5.0 %copy-start.3 = (bf16[4,8,10,384]{3,2,1,0:T(8,128)(2,1)S(1)}, bf16[4,8,10,384]{3,2,1,0:T(8,128)(2,1)}, u32[]{:S(2)}) copy-start(bf16[4,8,10,384]{3,2,1,0:T(8,128)(2,1)} %get-tuple-element.68) | copy-start | bytes 737284
  346.0 2.6 copy-start.4
  348.7 3.1 copy-start.24
  349.5 3.6 copy-start.31
  351.0 3.5 copy-start.30
  351.0 3.5 copy-start.73
  353.1 1.7 copy-start.29
  353.1 1.7 copy-start.72
  354.5 1.0 copy-start.42
  354.9 1.0 copy-start.27
  354.9 1.1 copy-start.71
  355.5 1.0 copy-start.26
  355.5 1.1 copy-start.70
  356.0 1.0 copy-start.25
  356.0 1.1 copy-start.48
  356.6 1.0 copy-start.23
  356.6 1.1 copy-start.69
  357.0 1.0 copy-start.22
  357.0 1.1 copy-start.68
  357.7 1.1 copy-start.46
  358.1 1.1 copy-start.67
  358.7 1.0 copy-start.19
  358.7 1.1 copy-start.66
  359.2 1.0 copy-start.18
  359.2 1.1 copy-start.78
  359.8 1.1 copy-start.65
  360.3 1.0 copy-start.16
  360.3 1.1 copy-start.43
  360.9 1.1 copy-start.64
  361.3 1.1 copy-start.63
  362.0 1.1 copy-start.41
  362.4 1.1 copy-start.59
  363.0 1.1 copy-start.58
  364.5 1.0 copy-start.56
  364.9 1.0 copy-start.9
  365.0 1.1 copy-start.55
  365.5 1.1 copy-start.38
  366.0 1.0 copy-start.7
  366.0 1.1 copy-start.53
  (34 other events, 32.7 us)
Sparse Core Ops, SparseCore 0:
  9.2 44.1 all-gather.2
  67.9 38.7 all-gather.4
